TPU v7x, 32 devices: a whole 2x2x4 slice. The times are simulated.
32 devices in a mesh: groups: 2 (over x), chan: 16 (over z, y, core).
Axes of the slice: x: 2, y: 2, z: 4, core: 2. Of those that a mesh axis runs over, the one named last changes fastest.
Arguments:
- xz: bfloat16 [256, 2, 8192], P('groups', None, 'chan'), parts along dimension 0, may hold values from -6 to 6
- conv_state: bfloat16 [256, 3, 8192], P('groups', None, 'chan'), parts along dimension 0, may hold values from -6 to 6
- conv_weight: float32 [4, 8192], P(None, 'chan'), may hold values from -3 to 3
- conv_bias: float32 [8192], P('chan'), may hold values from -3 to 3
- ssm_state: bfloat16 [256, 16, 8192], P('groups', None, 'chan'), parts along dimension 0, may hold values from -6 to 6
- x_weight: bfloat16 [8192, 544], P('chan'), may hold values from -0.0625 to 0.0625
- dt_weight: bfloat16 [512, 8192], P(None, 'chan'), may hold values from -0.25 to 0.25
- dt_bias: float32 [8192], P('chan'), may hold values from -4 to -1
- a_log: float32 [16, 8192], P(None, 'chan'), may hold values from -1 to 2.5
- d_skip: float32 [8192], P('chan'), may hold values from 0.5 to 1.5
- out_weight: bfloat16 [8192, 4096], P('chan'), may hold values from -0.0625 to 0.0625
- residual: bfloat16 [256, 4096], P(('groups', 'chan')), parts along dimension 0, may hold values from -6 to 6
- norm_gain: float32 [4096], replicated, may hold values from 0.5 to 1.5
- expert_ids: int32 [256, 2], P(('groups', 'chan')), parts along dimension 0, may hold values from 0 to 15, all different within a row; in each aligned block of 8 rows (0 to 7, 8 to 15, ...) at most 4 rows name the same one
- route_weight: float32 [256, 2], P(('groups', 'chan')), parts along dimension 0, may hold values from 0.2 to 1
- w_gate: bfloat16 [4096, 24576], P(None, 'chan'), may hold values from -0.09375 to 0.09375
- w_up: bfloat16 [4096, 24576], P(None, 'chan'), may hold values from -0.09375 to 0.09375
- w_down: bfloat16 [24576, 4096], P('chan'), may hold values from -0.0546875 to 0.0546875
Outputs:
- result: bfloat16 [256, 4096], P(('groups', 'chan')), parts along dimension 0
- new_state: bfloat16 [256, 16, 8192], P('groups', None, 'chan'), parts along dimension 0
There are 2 independent parts, one for each index of `groups`. A program takes and returns all parts, laid end to end along the dimension named above; an argument that names none is the same for every part. Nothing has to cross between parts.
Inputs may be any that keep to these rules, and one draw needn't show every extreme that they name: `expert_ids`: among the rows of one device, no expert is named by more than 4 rows.
All inputs are finite; a program needn't handle non-finite values.
Results may differ from a plain program's by a relative error of at most 0.006.
Values may be sent and summed in bfloat16 or wider, within the bound.
A program may use at most 128 MiB of HBM per device.

v0:
```python
import jax
import jax.numpy as jnp
from jax import lax
from jax.sharding import PartitionSpec as P

FLIGHT = 2


def expert_rows(rows, w_gate, w_up, w_down):
    gate = jnp.dot(rows, w_gate, preferred_element_type=jnp.float32)
    upper = jnp.dot(rows, w_up, preferred_element_type=jnp.float32)
    act = (jax.nn.silu(gate) * upper).astype(jnp.bfloat16)
    return jnp.dot(act, w_down, preferred_element_type=jnp.float32)


def shards(
    xz,
    conv_state,
    conv_weight,
    conv_bias,
    ssm_state,
    x_weight,
    dt_weight,
    dt_bias,
    a_log,
    d_skip,
    out_weight,
    residual,
    norm_gain,
    expert_ids,
    route_weight,
    w_gate,
    w_up,
    w_down,
):
    devices = lax.axis_size("chan")
    my_index = lax.axis_index("chan")
    per_expert = devices // FLIGHT
    my_expert = my_index // per_expert
    row_dev = residual.shape[0]
    rank_cols = dt_weight.shape[0]
    nstate = a_log.shape[0]
    x_new = xz[:, 0, :].astype(jnp.float32)
    gate_z = xz[:, 1, :].astype(jnp.float32)
    window = jnp.concatenate([conv_state.astype(jnp.float32), x_new[:, None, :]], axis=1)
    conv_out = jnp.sum(window * conv_weight[None, :, :], axis=1) + conv_bias
    u_mixer = jax.nn.silu(conv_out).astype(jnp.bfloat16)
    proj = lax.psum(jnp.dot(u_mixer, x_weight, preferred_element_type=jnp.float32), "chan")
    dt_low = proj[:, :rank_cols].astype(jnp.bfloat16)
    b_in = proj[:, rank_cols : rank_cols + nstate]
    c_out = proj[:, rank_cols + nstate :]
    step_size = jax.nn.softplus(
        jnp.dot(dt_low, dt_weight, preferred_element_type=jnp.float32) + dt_bias
    )
    rates = -jnp.exp(a_log)
    u_float = u_mixer.astype(jnp.float32)
    decay = jnp.exp(step_size[:, None, :] * rates[None, :, :])
    state = (
        decay * ssm_state.astype(jnp.float32) + (step_size * u_float)[:, None, :] * b_in[:, :, None]
    )
    y_mixer = jnp.sum(state * c_out[:, :, None], axis=1) + d_skip * u_float
    y_mixer = (y_mixer * jax.nn.silu(gate_z)).astype(jnp.bfloat16)
    new_state = state.astype(jnp.bfloat16)
    mixed_all = lax.psum(jnp.dot(y_mixer, out_weight, preferred_element_type=jnp.float32), "chan")
    mixed = lax.dynamic_slice_in_dim(mixed_all, my_index * row_dev, row_dev, 0)
    hidden = residual.astype(jnp.float32) + mixed
    scale = lax.rsqrt(jnp.mean(hidden * hidden, axis=-1, keepdims=True) + 1e-06)
    normed = (hidden * scale * norm_gain).astype(jnp.bfloat16)
    all_normed, all_ids, all_weights = (
        lax.all_gather(normed, "chan", axis=0, tiled=True),
        lax.all_gather(expert_ids, "chan", axis=0, tiled=True),
        lax.all_gather(route_weight.astype(jnp.bfloat16), "chan", axis=0, tiled=True).astype(
            route_weight.dtype
        ),
    )
    all_coef = jnp.sum(jnp.where(all_ids == my_expert, all_weights, jnp.float32(0.0)), axis=1)
    moe = lax.psum_scatter(
        all_coef[:, None] * expert_rows(all_normed, w_gate, w_up, w_down),
        "chan",
        scatter_dimension=0,
        tiled=True,
    )
    result = (hidden + moe).astype(jnp.bfloat16)
    return (result, new_state)


def solution(mesh):
    in_specs = (
        P("groups", None, "chan"),
        P("groups", None, "chan"),
        P(None, "chan"),
        P("chan"),
        P("groups", None, "chan"),
        P("chan", None),
        P(None, "chan"),
        P("chan"),
        P(None, "chan"),
        P("chan"),
        P("chan", None),
        P(("groups", "chan"), None),
        P(),
        P(("groups", "chan"), None),
        P(("groups", "chan"), None),
        P(None, "chan"),
        P(None, "chan"),
        P("chan", None),
    )
    out_specs = (P(("groups", "chan"), None), P("groups", None, "chan"))
    return jax.shard_map(shards, mesh=mesh, in_specs=in_specs, out_specs=out_specs, check_vma=False)
```

profile of v0, /device:TPU:0, one launch (start us, length us, event | category | flops | bytes accessed | tf_op | source)
XLA Modules:
  0.0 338.5 jit_solution(6719887400071741163)
XLA Ops:
  7.3 1.6 fusion.18
  8.9 1.1 multiply_reduce_fusion.1
  10.1 1.7 fusion.16
  11.8 0.0 all-reduce.5.cloned.1.call-start
  11.9 92.2 %all-reduce.3.cloned.1.call-done = f32[128,544]{0,1:T(8,128)} async-done(((f32[128,544]{0,1:T(8,128)}), f32[128,544]{0,1:T(8,128)}) %all-reduce.3.cloned.1.call-update) | async-done | bytes 278544 | tf_op jit(solution)/shard_map/psum | solution.py:48
  104.1 0.7 fusion.17
  104.9 0.1 copy.29
  105.0 0.1 copy.30
  105.1 1.7 convert_multiply_fusion.2
  106.8 2.9 fusion
  109.7 2.1 fusion.9
  111.9 0.0 all-gather.4.cloned.1.call-start
  111.9 97.6 %all-reduce.5.cloned.1.call-done = f32[128,4096]{1,0:T(8,128)} async-done(((f32[128,4096]{1,0:T(8,128)}), f32[128,4096]{1,0:T(8,128)}) %all-reduce.5.cloned.1.call-update) | async-done | bytes 2097168 | tf_op jit(solution)/shard_map/psum | solution.py:64
  209.6 1.1 multiply_reduce_fusion.2
  210.6 1.6 multiply_convert_fusion.1
  212.3 0.0 reduce-scatter.2.cloned.1.call-start
  212.4 19.6 %all-gather.1 = bf16[16,8,2]{1,2,0:T(2,128)(2,1)S(1)} all-gather(bf16[1,8,2]{1,2,0:T(2,128)(2,1)S(1)} %convert_bitcast_fusion), channel_id=1, replica_groups=mesh['groups'=2,'chan'=16] {'chan'}, dimensions={0}, use_global_device_ids=true | all-gather | bytes 544 | tf_op jit(solution)/shard_map/all_gather | solution.py:72
  231.9 17.4 %all-gather = s32[16,8,2]{1,2,0:T(2,128)S(1)} all-gather(s32[1,8,2]{1,2,0:T(2,128)S(1)} %bitcast.17), channel_id=1, replica_groups=mesh['groups'=2,'chan'=16] {'chan'}, dimensions={0}, use_global_device_ids=true | all-gather | bytes 1088 | tf_op jit(solution)/shard_map/all_gather | solution.py:71
  249.4 0.1 reshape.35
  249.5 0.3 all-gather.4.cloned.1.call-done
  249.7 6.8 %fusion.19 = f32[128,1536]{1,0:T(8,128)S(1)} fusion(bf16[128,4096]{1,0:T(8,128)(2,1)} %all-gather.4.cloned.1.call-done, bf16[4096,1536]{1,0:T(8,128)(2,1)} %param.33), kind=kOutput, calls=%fused_computation.40 | convolution fusion | flops 1610612736 | bytes 14417920 | tf_op jit(solution)/shard_map/dot_general | solution.py:10
  256.5 13.1 %convolution_multiply_fusion = f32[128,4096]{1,0:T(8,128)} fusion(bf16[1536,4096]{1,0:T(8,128)(2,1)} %param.35, f32[128]{0:T(128)S(1)} %reshape.35, bf16[128,4096]{1,0:T(8,128)(2,1)S(1)} %copy-done.1, bf16[4096,1536]{1,0:T(8,128)(2,1)} %param.34, f32[128,1536]{1,0:T(8,128)S(1)} %fusion.19), kind=kOutput, calls=%fused_computation | convolution fusion | flops 3222929408 | bytes 29098496 | tf_op jit(solution)/shard_map/dot_general | solution.py:13
  269.7 60.7 %reduce-scatter.2.cloned.1.call-done = f32[8,4096]{1,0:T(8,128)} async-done(((f32[128,4096]{1,0:T(8,128)}), f32[8,4096]{1,0:T(8,128)}) %reduce-scatter.2.cloned.1.call-update) | async-done | bytes 131088 | tf_op jit(solution)/shard_map/reduce_scatter | solution.py:77
  330.4 1.6 add_convert_fusion
  (34 shorter events, 0.2 us)
Async XLA Ops:
  7.2 2.9 copy-start
  7.2 97.9 %copy-start.7 = (f32[512]{0:T(512)S(1)}, f32[512]{0:T(512)}, u32[]{:S(2)}) copy-start(f32[512]{0:T(512)} %param.21) | copy-start | bytes 6148
  7.2 4.7 %copy-start.5 = (f32[16,512]{1,0:T(8,128)S(1)}, f32[16,512]{1,0:T(8,128)}, u32[]{:S(2)}) copy-start(f32[16,512]{1,0:T(8,128)} %param.26) | copy-start | bytes 98308
  7.2 97.9 %copy-start.10 = (f32[512]{0:T(512)S(1)}, f32[512]{0:T(512)}, u32[]{:S(2)}) copy-start(f32[512]{0:T(512)} %param.25) | copy-start | bytes 6148
  7.2 99.6 %copy-start.3 = (bf16[128,16,512]{2,1,0:T(8,128)(2,1)S(1)}, bf16[128,16,512]{2,1,0:T(8,128)(2,1)}, u32[]{:S(2)}) copy-start(bf16[128,16,512]{2,1,0:T(8,128)(2,1)} %param.22) | copy-start | bytes 6291460
  7.2 96.9 %all-reduce.3.cloned.1.call-start = ((), (), s32[]{:S(2)}) async-start(), calls=%async_computation.1 | async-start | bytes 557056 | tf_op jit(solution)/shard_map/psum | solution.py:48
  11.8 97.8 %copy-start.8 = (f32[512]{0:T(512)S(1)}, f32[512]{0:T(512)}, u32[]{:S(2)}) copy-start(f32[512]{0:T(512)} %param.27) | copy-start | bytes 6148
  11.8 197.7 %all-reduce.5.cloned.1.call-start = ((), (), s32[]{:S(2)}) async-start(), calls=%async_computation.2 | async-start | bytes 4194304 | tf_op jit(solution)/shard_map/psum | solution.py:64
  105.1 4.6 %copy-start.2 = (bf16[512,4096]{1,0:T(8,128)(2,1)S(1)}, bf16[512,4096]{1,0:T(8,128)(2,1)}, u32[]{:S(2)}) copy-start(bf16[512,4096]{1,0:T(8,128)(2,1)} %param.28) | copy-start | bytes 12582916
  109.7 99.9 %copy-start.4 = (bf16[8,4096]{1,0:T(8,128)(2,1)S(1)}, bf16[8,4096]{1,0:T(8,128)(2,1)}, u32[]{:S(2)}) copy-start(bf16[8,4096]{1,0:T(8,128)(2,1)} %param.29) | copy-start | bytes 196612
  109.7 100.9 %copy-start.6 = (f32[4096]{0:T(1024)S(1)}, f32[4096]{0:T(1024)}, u32[]{:S(2)}) copy-start(f32[4096]{0:T(1024)} %param.30) | copy-start | bytes 49156
  109.7 102.7 %copy-start.11 = (f32[8,2]{0,1:T(2,128)S(1)}, f32[8,2]{0,1:T(2,128)}, u32[]{:S(2)}) copy-start(f32[8,2]{0,1:T(2,128)} %param.32) | copy-start | bytes 196
  109.7 122.3 %copy-start.9 = (s32[8,2]{0,1:T(2,128)S(1)}, s32[8,2]{0,1:T(2,128)}, u32[]{:S(2)}) copy-start(s32[8,2]{0,1:T(2,128)} %param.31) | copy-start | bytes 196
  111.9 137.8 %all-gather.4.cloned.1.call-start = ((), (), s32[]{:S(2)}) async-start(), calls=%async_computation.3 | async-start | bytes 1114112 | tf_op jit(solution)/shard_map/all_gather | solution.py:70
  212.3 118.1 %reduce-scatter.2.cloned.1.call-start = ((), (), s32[]{:S(2)}) async-start(), calls=%async_computation.4 | async-start | bytes 2228224 | tf_op jit(solution)/shard_map/reduce_scatter | solution.py:77
  249.7 6.8 %copy-start.1 = (bf16[128,4096]{1,0:T(8,128)(2,1)S(1)}, bf16[128,4096]{1,0:T(8,128)(2,1)}, u32[]{:S(2)}) copy-start(bf16[128,4096]{1,0:T(8,128)(2,1)} %all-gather.4.cloned.1.call-done) | copy-start | bytes 3145732
Sparse Core Ops, SparseCore 0:
  12.0 92.0 all-reduce.2
  112.0 97.5 all-reduce.4
  212.5 37.1 all-gather.3
  269.8 60.5 reduce-scatter.1
where the time goes:
time: 339 us
  waiting for transfers between devices  251 us (74%)
  blocking collectives  37 us (11%)
  matrix products  25.5 us (8%)
  between operations  14 us (4%)
  other arithmetic  8.34 us (2%)
    psum x1, waiting for transfers between devices, shards(): lax.psum(jnp.dot(y_mixer, out_weight, preferred_element_type=jnp.float32)...  97.6 us
    psum x1, waiting for transfers between devices, shards(): lax.psum(jnp.dot(u_mixer, x_weight, preferred_element_type=jnp.float32),...  92.2 us
    reduce_scatter x1, waiting for transfers between devices, shards(): lax.psum_scatter(all_coef[:, None] * expert_rows(all_normed, w_gate, w_up...  60.7 us
    all_gather x1, blocking collectives, shards(): lax.all_gather(route_weight.astype(jnp.bfloat16), 'chan', axis=0, tiled=T...  19.6 us
    all_gather x1, blocking collectives, shards(): lax.all_gather(expert_ids, 'chan', axis=0, tiled=True)  17.4 us
    dot_general x1, matrix products, expert_rows(): return jnp.dot(act, w_down, preferred_element_type=jnp.float32)  13.1 us
  transfers between devices with their start and end apart: 4, of which 4 were waited for; matrix products, arithmetic and copies ran while one was open for 0% of the time, Pallas kernels for 0%

commit v1 on v0

v1 whole, which is shorter than its diff:
```python
import functools

import jax
import jax.numpy as jnp
from jax import lax
from jax.experimental import pallas as pl
from jax.experimental.pallas import tpu as pltpu
from jax.sharding import PartitionSpec as P

FLIGHT = 2
CAP = 4
PACK = 4
MESH = pl.DeviceIdType.MESH


def push(src, dst, send_sem, recv_sem, peer):
    return pltpu.make_async_remote_copy(
        src_ref=src,
        dst_ref=dst,
        send_sem=send_sem,
        recv_sem=recv_sem,
        device_id={"chan": peer},
        device_id_type=MESH,
    )


def proj_kernel(n, part_ref, out_ref, landed, full, send_a, recv_a, send_b, recv_b):
    me = lax.axis_index("chan")
    barrier = pltpu.get_barrier_semaphore()

    @pl.loop(1, n)
    def _(k):
        pl.semaphore_signal(barrier, inc=1, device_id={"chan": (me + k) % n}, device_id_type=MESH)

    pl.semaphore_wait(barrier, n - 1)

    def scatter(owner, sender, peer):
        return push(part_ref.at[owner], landed.at[sender], send_a.at[owner], recv_a.at[sender], peer)

    def gather(slot, peer, sem):
        return push(full.at[slot], full.at[slot], send_b.at[sem], recv_b.at[slot], peer)

    @pl.loop(1, n)
    def _(k):
        peer = (me + k) % n
        scatter(peer, me, peer).start()

    def add(k, total):
        peer = (me + n - k) % n
        scatter(peer, peer, peer).wait_recv()
        return total + landed[peer].astype(jnp.float32)

    total = lax.fori_loop(1, n, add, part_ref[me].astype(jnp.float32))
    full[me] = total.astype(jnp.bfloat16)

    @pl.loop(1, n)
    def _(k):
        peer = (me + k) % n
        gather(me, peer, peer).start()

    @pl.loop(1, n)
    def _(k):
        peer = (me + n - k) % n
        gather(peer, peer, peer).wait_recv()

    out_ref[...] = full[...]

    @pl.loop(1, n)
    def _(k):
        peer = (me + k) % n
        scatter(peer, me, peer).wait_send()
        gather(me, peer, peer).wait_send()


def sum_proj(part, n):
    rows, cols = part.shape[1:]
    vmem = pl.BlockSpec(memory_space=pltpu.VMEM)
    return pl.pallas_call(
        functools.partial(proj_kernel, n),
        out_shape=jax.ShapeDtypeStruct(part.shape, jnp.bfloat16),
        in_specs=[vmem],
        out_specs=vmem,
        scratch_shapes=[
            pltpu.VMEM((n, rows, cols), jnp.bfloat16),
            pltpu.VMEM((n, rows, cols), jnp.bfloat16),
        ]
        + [pltpu.SemaphoreType.DMA((n,))] * 4,
        compiler_params=pltpu.CompilerParams(
            collective_id=0, has_side_effects=True, vmem_limit_bytes=16 * 2**20
        ),
    )(part)


def moe_kernel(
    n,
    y_ref,
    out_weight,
    residual_ref,
    gain_ref,
    ids_ref,
    ids_t_ref,
    route_ref,
    w_gate,
    w_up,
    w_down,
    result_ref,
    v_out,
    v_gate,
    v_up,
    v_down,
    part,
    own,
    pair_in,
    summed,
    mixed_in,
    hidden_ref,
    picked_f,
    picked,
    rows_in,
    rows,
    act,
    back_f,
    back,
    back_in,
    back_sum,
    final_in,
    local_sem,
    pair_sem,
    mixed_send,
    mixed_recv,
    rows_send,
    rows_recv,
    forward_send,
    final_send,
    final_recv,
):
    chips = n // 2
    half = chips // FLIGHT
    me = lax.axis_index("chan")
    chip, core = me // 2, me % 2
    other = 1 - core
    partner = chip * 2 + other
    row_dev, width = residual_ref.shape
    piece = width // PACK
    block = CAP * PACK
    f32, bf16 = jnp.float32, jnp.bfloat16

    load_out = pltpu.make_async_copy(out_weight, v_out, local_sem.at[0])
    loads = [
        pltpu.make_async_copy(src, dst, local_sem.at[i + 1])
        for i, (src, dst) in enumerate([(w_gate, v_gate), (w_up, v_up), (w_down, v_down)])
    ]
    load_out.start()

    barrier = pltpu.get_barrier_semaphore()
    pl.semaphore_signal(barrier, inc=1, device_id={"chan": partner}, device_id_type=MESH)

    @pl.loop(1, chips)
    def _(k):
        peer = ((chip + k) % chips) * 2 + core
        pl.semaphore_signal(barrier, inc=1, device_id={"chan": peer}, device_id_type=MESH)

    load_out.wait()
    for load in loads:
        load.start()

    tile = 512
    y_other = y_ref[other]

    @pl.loop(0, width // tile)
    def _(t):
        cols = pl.ds(pl.multiple_of(t * tile, tile), tile)
        value = jnp.dot(y_other, v_out[:, cols], preferred_element_type=f32)
        part[:, :, cols] = value.reshape(chips, row_dev, tile).astype(bf16)

    pl.semaphore_wait(barrier, chips)
    pair = push(part, pair_in, pair_sem.at[0], pair_sem.at[1], partner)
    pair.start()
    y_own = y_ref[core]

    @pl.loop(0, width // tile)
    def _(t):
        cols = pl.ds(pl.multiple_of(t * tile, tile), tile)
        value = jnp.dot(y_own, v_out[:, cols], preferred_element_type=f32)
        own[:, :, cols] = value.reshape(chips, row_dev, tile)

    pair.wait_recv()

    def mixed_copy(owner, sender):
        return push(
            summed.at[owner], mixed_in.at[sender], mixed_send.at[owner], mixed_recv.at[sender],
            owner * 2 + core,
        )

    @pl.loop(1, chips)
    def _(k):
        owner = (chip + k) % chips
        summed[owner] = (own[owner] + pair_in[owner].astype(f32)).astype(bf16)
        mixed_copy(owner, chip).start()

    hidden_ref[...] = residual_ref[...].astype(f32) + own[chip] + pair_in[chip].astype(f32)

    @pl.loop(1, chips)
    def _(k):
        sender = (chip + chips - k) % chips
        push(
            summed.at[sender], mixed_in.at[sender], mixed_send.at[sender], mixed_recv.at[sender],
            sender * 2 + core,
        ).wait_recv()
        hidden_ref[...] += mixed_in[sender].astype(f32)

    hidden = hidden_ref[...]
    scale = lax.rsqrt(jnp.mean(hidden * hidden, axis=-1, keepdims=True) + 1e-06)
    normed = (hidden * scale * gain_ref[...]).astype(bf16).astype(f32)

    ids, ids_t, route = ids_ref[...], ids_t_ref[...], route_ref[...]
    earlier = lax.broadcasted_iota(jnp.int32, (row_dev, row_dev), 1) < lax.broadcasted_iota(
        jnp.int32, (row_dev, row_dev), 0
    )
    masks = []
    for e in range(FLIGHT):
        named = jnp.where((ids[:, 0:1] == e) | (ids[:, 1:2] == e), 1.0, 0.0)
        named_row = jnp.where((ids_t[0:1, :] == e) | (ids_t[1:2, :] == e), 1.0, 0.0)
        place = jnp.sum(jnp.where(earlier, named_row, 0.0), axis=1, keepdims=True)
        masks.append([jnp.where(place == float(r), named, 0.0) for r in range(CAP)])
        for r in range(CAP):
            row = jnp.sum(masks[e][r] * normed, axis=0, keepdims=True)
            for q in range(PACK):
                at = q * CAP + r
                picked_f[e, at : at + 1, :] = row[:, q * piece : (q + 1) * piece]
    picked[...] = picked_f[...].astype(bf16)

    def rows_copy(slot_core, sender, peer_chip, peer_core, expert, sem):
        slot = slot_core * chips + sender
        return push(
            picked.at[expert], rows_in.at[slot], rows_send.at[sem], rows_recv.at[slot],
            peer_chip * 2 + peer_core,
        )

    def forward(sender, slot_core):
        slot = slot_core * chips + sender
        return push(
            rows_in.at[slot], rows_in.at[slot], forward_send.at[sender], rows_recv.at[slot], partner
        )

    my_expert = chip // half

    @pl.loop(1, chips)
    def _(k):
        peer = (chip + k) % chips
        rows_copy(core, chip, peer, core, peer // half, peer).start()

    rows_copy(core, chip, chip, other, my_expert, chip).start()
    rows_in[core * chips + chip] = picked[my_expert]

    @pl.loop(1, chips)
    def _(k):
        sender = (chip + chips - k) % chips
        rows_copy(core, sender, chip, other, my_expert, sender).wait_recv()
        forward(sender, core).start()

    @pl.loop(0, chips)
    def _(k):
        sender = (chip + chips - k) % chips
        forward(sender, other).wait_recv()

    count = n * CAP
    from_row = lax.broadcasted_iota(jnp.int32, (count, n * block), 0)
    from_col = lax.broadcasted_iota(jnp.int32, (count, n * block), 1)
    to_row = lax.broadcasted_iota(jnp.int32, (n * block, count), 1)
    to_col = lax.broadcasted_iota(jnp.int32, (n * block, count), 0)

    def packed_at(row, q):
        return (row // CAP) * block + q * CAP + row % CAP

    flat = rows_in[...].reshape(n * block, piece)
    for q in range(PACK):
        pick = jnp.where(from_col == packed_at(from_row, q), 1.0, 0.0).astype(bf16)
        rows[:, q * piece : (q + 1) * piece] = jnp.dot(
            pick, flat, preferred_element_type=f32
        ).astype(bf16)

    loads[0].wait()
    loads[1].wait()
    units = v_gate.shape[1]
    span = 512 if units % 512 == 0 else units

    @pl.loop(0, units // span)
    def _(t):
        cols = pl.ds(pl.multiple_of(t * span, span), span)
        gate = jnp.dot(rows[...], v_gate[:, cols], preferred_element_type=f32)
        upper = jnp.dot(rows[...], v_up[:, cols], preferred_element_type=f32)
        act[:, cols] = (jax.nn.silu(gate) * upper).astype(bf16)

    loads[2].wait()
    for q in range(PACK):
        out = jnp.dot(
            act[...], v_down[:, q * piece : (q + 1) * piece], preferred_element_type=f32
        ).astype(bf16)
        pick = jnp.where(to_col == packed_at(to_row, q), 1.0, 0.0).astype(bf16)
        moved = jnp.dot(pick, out, preferred_element_type=f32)
        if q == 0:
            back_f[...] = moved
        else:
            back_f[...] += moved
    back[...] = back_f[...].reshape(2, chips, block, piece).astype(bf16)

    swap = push(back.at[other], back_in, pair_sem.at[2], pair_sem.at[3], partner)
    swap.start()
    swap.wait_recv()

    def final_copy(owner, sender, peer):
        return push(
            back_sum.at[owner], final_in.at[sender], final_send.at[owner], final_recv.at[sender],
            peer * 2 + core,
        )

    @pl.loop(1, chips)
    def _(k):
        owner = (chip + k) % chips
        back_sum[owner] = (back[core, owner].astype(f32) + back_in[owner].astype(f32)).astype(bf16)
        final_copy(owner, chip, owner).start()

    final_in[chip] = (back[core, chip].astype(f32) + back_in[chip].astype(f32)).astype(bf16)

    @pl.loop(1, chips)
    def _(k):
        sender = (chip + chips - k) % chips
        final_copy(sender, sender, sender).wait_recv()

    hidden = hidden_ref[...]
    for e in range(FLIGHT):
        coef = jnp.sum(jnp.where(ids == e, route, 0.0), axis=1, keepdims=True)
        total = jnp.sum(final_in[e * half : (e + 1) * half].astype(f32), axis=0)
        weights = [coef * masks[e][r] for r in range(CAP)]
        if e == 0:
            moe = [None] * PACK
        for q in range(PACK):
            for r in range(CAP):
                at = q * CAP + r
                term = weights[r] * total[at : at + 1, :]
                moe[q] = term if moe[q] is None else moe[q] + term
    for q in range(PACK):
        cols = slice(q * piece, (q + 1) * piece)
        result_ref[:, cols] = (hidden[:, cols] + moe[q]).astype(bf16)

    pair.wait_send()
    swap.wait_send()
    rows_copy(core, chip, chip, other, my_expert, chip).wait_send()

    @pl.loop(1, chips)
    def _(k):
        peer = (chip + k) % chips
        mixed_copy(peer, chip).wait_send()
        rows_copy(core, chip, peer, core, peer // half, peer).wait_send()
        forward(peer, core).wait_send()
        final_copy(peer, chip, peer).wait_send()


def mix_experts(y, out_weight, residual, gain, ids, route, w_gate, w_up, w_down, n):
    chips = n // 2
    row_dev, width = residual.shape
    piece, block = width // PACK, CAP * PACK
    vmem, hbm = pl.BlockSpec(memory_space=pltpu.VMEM), pl.BlockSpec(memory_space=pl.ANY)
    bf16, f32 = jnp.bfloat16, jnp.float32
    dma = pltpu.SemaphoreType.DMA
    return pl.pallas_call(
        functools.partial(moe_kernel, n),
        out_shape=jax.ShapeDtypeStruct((row_dev, width), bf16),
        in_specs=[vmem, hbm, vmem, vmem, vmem, vmem, vmem, hbm, hbm, hbm],
        out_specs=vmem,
        scratch_shapes=[
            pltpu.VMEM(out_weight.shape, bf16),
            pltpu.VMEM(w_gate.shape, bf16),
            pltpu.VMEM(w_up.shape, bf16),
            pltpu.VMEM(w_down.shape, bf16),
            pltpu.VMEM((chips, row_dev, width), bf16),
            pltpu.VMEM((chips, row_dev, width), f32),
            pltpu.VMEM((chips, row_dev, width), bf16),
            pltpu.VMEM((chips, row_dev, width), bf16),
            pltpu.VMEM((chips, row_dev, width), bf16),
            pltpu.VMEM((row_dev, width), f32),
            pltpu.VMEM((FLIGHT, block, piece), f32),
            pltpu.VMEM((FLIGHT, block, piece), bf16),
            pltpu.VMEM((n, block, piece), bf16),
            pltpu.VMEM((n * CAP, width), bf16),
            pltpu.VMEM((n * CAP, w_gate.shape[1]), bf16),
            pltpu.VMEM((n * block, piece), f32),
            pltpu.VMEM((2, chips, block, piece), bf16),
            pltpu.VMEM((chips, block, piece), bf16),
            pltpu.VMEM((chips, block, piece), bf16),
            pltpu.VMEM((chips, block, piece), bf16),
            dma((4,)),
            dma((4,)),
            dma((chips,)),
            dma((chips,)),
            dma((chips,)),
            dma((n,)),
            dma((chips,)),
            dma((chips,)),
            dma((chips,)),
        ],
        compiler_params=pltpu.CompilerParams(
            collective_id=1, has_side_effects=True, vmem_limit_bytes=60 * 2**20
        ),
    )(y, out_weight, residual, gain.reshape(1, width), ids, ids.T, route, w_gate, w_up, w_down)


def shards(
    xz,
    conv_state,
    conv_weight,
    conv_bias,
    ssm_state,
    x_weight,
    dt_weight,
    dt_bias,
    a_log,
    d_skip,
    out_weight,
    residual,
    norm_gain,
    expert_ids,
    route_weight,
    w_gate,
    w_up,
    w_down,
):
    devices = lax.axis_size("chan")
    row_dev = residual.shape[0]
    rank_cols = dt_weight.shape[0]
    nstate = a_log.shape[0]
    x_new = xz[:, 0, :].astype(jnp.float32)
    gate_z = xz[:, 1, :].astype(jnp.float32)
    window = jnp.concatenate([conv_state.astype(jnp.float32), x_new[:, None, :]], axis=1)
    conv_out = jnp.sum(window * conv_weight[None, :, :], axis=1) + conv_bias
    u_mixer = jax.nn.silu(conv_out).astype(jnp.bfloat16)
    part = jnp.dot(u_mixer, x_weight, preferred_element_type=jnp.float32).astype(jnp.bfloat16)
    proj = sum_proj(part.reshape(devices, row_dev, -1), devices).reshape(part.shape)
    proj = proj.astype(jnp.float32)
    dt_low = proj[:, :rank_cols].astype(jnp.bfloat16)
    b_in = proj[:, rank_cols : rank_cols + nstate]
    c_out = proj[:, rank_cols + nstate :]
    step_size = jax.nn.softplus(
        jnp.dot(dt_low, dt_weight, preferred_element_type=jnp.float32) + dt_bias
    )
    rates = -jnp.exp(a_log)
    u_float = u_mixer.astype(jnp.float32)
    decay = jnp.exp(step_size[:, None, :] * rates[None, :, :])
    state = (
        decay * ssm_state.astype(jnp.float32) + (step_size * u_float)[:, None, :] * b_in[:, :, None]
    )
    y_mixer = jnp.sum(state * c_out[:, :, None], axis=1) + d_skip * u_float
    y_mixer = (y_mixer * jax.nn.silu(gate_z)).astype(jnp.bfloat16)
    new_state = state.astype(jnp.bfloat16)
    y_halves = y_mixer.reshape(devices // 2, 2, row_dev, -1).transpose(1, 0, 2, 3)
    result = mix_experts(
        y_halves.reshape(2, devices // 2 * row_dev, -1),
        out_weight,
        residual,
        norm_gain,
        expert_ids,
        route_weight,
        w_gate,
        w_up,
        w_down,
        devices,
    )
    return (result, new_state)


def solution(mesh):
    in_specs = (
        P("groups", None, "chan"),
        P("groups", None, "chan"),
        P(None, "chan"),
        P("chan"),
        P("groups", None, "chan"),
        P("chan", None),
        P(None, "chan"),
        P("chan"),
        P(None, "chan"),
        P("chan"),
        P("chan", None),
        P(("groups", "chan"), None),
        P(),
        P(("groups", "chan"), None),
        P(("groups", "chan"), None),
        P(None, "chan"),
        P(None, "chan"),
        P("chan", None),
    )
    out_specs = (P(("groups", "chan"), None), P("groups", None, "chan"))
    return jax.shard_map(shards, mesh=mesh, in_specs=in_specs, out_specs=out_specs, check_vma=False)
```

time: 339 us -> 75.6 us (0.22)
  waiting for transfers between devices: 251 us -> 0 us
  Pallas kernels: 0 us -> 62.4 us
  blocking collectives: 37 us -> 0 us
  matrix products: 25.5 us -> 2.48 us
  between operations: 14 us -> 0.8 us
  other arithmetic: 8.34 us -> 4.8 us
    psum x2 -> x0, waiting for transfers between devices: 190 us -> none  [the longest x1 97.6 us: shards(): lax.psum(jnp.dot(y_mixer, out_weight, preferred_element_type=jnp.float32)...]
    pallas_call x0 -> x2, Pallas kernels: none -> 62.4 us  [the longest x1 45.5 us: mix_experts(): pl.pallas_call(functools.partial(moe_kernel, n), out_shape=jax.ShapeDtype...]
    reduce_scatter x1 -> x0, waiting for transfers between devices: 60.7 us -> none  [shards(): lax.psum_scatter(all_coef[:, None] * expert_rows(all_normed, w_gate, w_up...]
    all_gather x2 -> x0, blocking collectives: 37 us -> none  [the longest x1 19.6 us: shards(): lax.all_gather(route_weight.astype(jnp.bfloat16), 'chan', axis=0, tiled=T...]
    dot_general x3 -> x0, matrix products: 22.1 us -> none  [the longest x1 13.1 us: expert_rows(): return jnp.dot(act, w_down, preferred_element_type=jnp.float32)]
  transfers between devices with their start and end apart: 4 -> 0, of which waited for: 4 -> 0; matrix products, arithmetic and copies ran while one was open for 0% -> 0% of each run, Pallas kernels for 0% -> 0%
where the time goes in v1:
time: 75.6 us; the launch traced here: 75.3 us
  Pallas kernels  62.4 us (83%)
  other arithmetic  4.8 us (6%)
  local copies, waits for them, and re-layouts  4.79 us (6%)
  matrix products  2.48 us (3%)
  between operations  0.8 us (1%)
    pallas_call x1, Pallas kernels, mix_experts(): pl.pallas_call(functools.partial(moe_kernel, n), out_shape=jax.ShapeDtype...  45.5 us
    pallas_call x1, Pallas kernels, sum_proj(): pl.pallas_call(functools.partial(proj_kernel, n), out_shape=jax.ShapeDtyp...  16.9 us
    unnamed x21, local copies, waits for them, and re-layouts  2.91 us
    convert_element_type x1, other arithmetic, shards(): new_state = state.astype(jnp.bfloat16)  2.81 us
    slice x1, local copies, waits for them, and re-layouts, shards(): x_new = xz[:, 0, :].astype(jnp.float32)  1.64 us

profile of v1, /device:TPU:0, one launch (start us, length us, event | category | flops | bytes accessed | tf_op | source)
XLA Modules:
  0.0 75.3 jit_solution(12588311803732698223)
XLA Ops:
  0.6 0.0 copy-start
  0.6 0.0 copy-start.1
  0.7 0.0 copy-start.4
  0.7 0.0 copy-start.7
  0.7 0.0 copy-start.2
  0.7 1.6 %fusion.9 = (bf16[128,1,512]{2,1,0:T(2,128)(2,1)S(1)}, bf16[128,1,512]{2,1,0:T(2,128)(2,1)S(1)}) fusion(bf16[128,2,512]{2,1,0:T(2,128)(2,1)} %param.18), kind=kLoop, calls=%fused_computation.23 | loop fusion | bytes 524288 | tf_op jit(solution)/shard_map/slice | solution.py:433
  2.4 1.1 %multiply_reduce_fusion.1 = f32[128,512]{1,0:T(8,128)S(1)} fusion(bf16[128,1,512]{2,0,1:T(8,128)(2,1)S(1)} %copy.33, bf16[128,3,512]{2,0,1:T(8,128)(2,1)} %param.19, f32[4,512]{1,0:T(4,128)} %param.20), kind=kLoop, calls=%fused_computation.5 | loop fusion | flops 983040 | bytes 794624 | tf_op jit(solution)/shard_map/reduce_sum | solution.py:436
  3.5 1.0 %convolution_convert_fusion = bf16[128,544]{0,1:T(8,128)(2,1)S(1)} fusion(bf16[512,544]{0,1:T(8,128)(2,1)S(1)} %copy-done, f32[128,512]{1,0:T(8,128)S(1)} %multiply_reduce_fusion.1, f32[512]{0:T(512)} %param.21), kind=kOutput, calls=%fused_computation.4 | convolution fusion | flops 71766016 | bytes 960512 | tf_op jit(solution)/shard_map/dot_general | solution.py:438
  4.6 0.2 copy.28
  4.7 16.9 %shard_map.185 = bf16[16,8,544]{2,1,0:T(8,128)(2,1)S(1)} custom-call(bf16[16,8,544]{2,1,0:T(8,128)(2,1)S(1)} %bitcast.16), custom_call_target="tpu_custom_call" | custom-call | tf_op jit(solution)/shard_map/pallas_call | solution.py:78
  21.7 0.0 copy-start.5
  21.7 0.1 fusion.8
  21.8 0.0 copy-done.7
  21.8 0.0 copy-start.3
  21.9 0.0 copy-start.6
  21.9 1.4 %convert_multiply_fusion.1 = (f32[128,512]{1,0:T(8,128)S(1)}, f32[128,512]{1,0:T(8,128)S(1)}) fusion(f32[128,512]{1,0:T(8,128)S(1)} %multiply_reduce_fusion.1, f32[512]{0:T(512)S(1)} %copy-done.4, f32[512]{0:T(512)S(1)} %copy-done.7, bf16[512,512]{1,0:T(8,128)(2,1)} %param.24, bf16[128,544]{1,0:T(8,128)(2,1)S(1)} %bitcast.17), kind=kOutput, calls=%fused_computation.14 | convolution fusion | flops 68091904 | bytes 1445888 | tf_op jit(solution)/shard_map/dot_general | solution.py:445
  23.3 0.0 copy-done.1
  23.4 2.8 %fusion = (bf16[128,16,512]{2,1,0:T(8,128)(2,1)}, f32[128,512]{1,0:T(8,128)S(1)}) fusion(bf16[128,16,512]{2,1,0:T(8,128)(2,1)S(1)} %copy-done.1, f32[128,16]{1,0:T(8,128)S(1)} %get-tuple-element.4, f32[128,512]{1,0:T(8,128)S(1)} %get-tuple-element.8, f32[16,512]{1,0:T(8,128)S(1)} %exponential_negate_fusion, f32[128,512]{1,0:T(8,128)S(1)} %get-tuple-element.9, ...), kind=kLoop, calls=%fused_computation.2 | loop fusion | flops 8323072 | bytes 5029888 | tf_op jit(solution)/shard_map/convert_element_type | solution.py:455
  26.2 0.0 copy-done.5
  26.2 0.8 %copy_bitcast_fusion.y_ref = bf16[2,64,512]{2,1,0:T(8,128)(2,1)} fusion(bf16[8,2,8,512]{3,2,1,0:T(8,128)(2,1)S(1)} %bitcast.20, f32[8,2,8,512]{3,2,1,0:T(8,128)S(1)} %bitcast.19, f32[8,2,8,512]{3,2,1,0:T(8,128)S(1)} %bitcast.18, f32[512]{0:T(512)S(1)} %copy-done.4, f32[512]{0:T(512)S(1)} %copy-done.5), kind=kLoop, calls=%fused_computation.18 | loop fusion | flops 1048576 | bytes 790528 | tf_op jit(solution)/shard_map/reshape | solution.py:458
  27.0 0.7 copy.31.ids_ref
  27.7 0.7 copy.32.route_ref
  28.3 45.5 %shard_map.186 = bf16[8,4096]{1,0:T(8,128)(2,1)} custom-call(bf16[2,64,512]{2,1,0:T(8,128)(2,1)} %copy_bitcast_fusion.y_ref, bf16[512,4096]{1,0:T(8,128)(2,1)} %out_weight.1, bf16[8,4096]{1,0:T(8,128)(2,1)} %residual_ref.1, f32[1,4096]{1,0:T(1,128)} %bitcast.21, s32[8,2]{1,0:T(8,128)} %copy.31.ids_ref, s32[2,8]{1,0:T(2,128)} %bitcast.22, ...), custom_call_target="tpu_custom_call" | custom-call | tf_op jit(solution)/shard_map/pallas_call | solution.py:367
  73.8 1.5 %copy.37 = bf16[8,4096]{1,0:T(8,128)(2,1)} copy(bf16[8,4096]{1,0:T(8,128)(2,1)} %shard_map.186) | data formatting | bytes 131072
  (9 shorter events, 0.1 us)
Async XLA Ops:
  0.6 2.9 %copy-start = (bf16[512,544]{0,1:T(8,128)(2,1)S(1)}, bf16[512,544]{0,1:T(8,128)(2,1)}, u32[]{:S(2)}) copy-start(bf16[512,544]{0,1:T(8,128)(2,1)} %param.23) | copy-start | bytes 1671172
  0.6 22.7 %copy-start.1 = (bf16[128,16,512]{2,1,0:T(8,128)(2,1)S(1)}, bf16[128,16,512]{2,1,0:T(8,128)(2,1)}, u32[]{:S(2)}) copy-start(bf16[128,16,512]{2,1,0:T(8,128)(2,1)} %param.22) | copy-start | bytes 6291460
  0.7 21.2 %copy-start.4 = (f32[512]{0:T(512)S(1)}, f32[512]{0:T(512)}, u32[]{:S(2)}) copy-start(f32[512]{0:T(512)} %param.21) | copy-start | bytes 6148
  0.7 21.2 %copy-start.7 = (f32[512]{0:T(512)S(1)}, f32[512]{0:T(512)}, u32[]{:S(2)}) copy-start(f32[512]{0:T(512)} %param.25) | copy-start | bytes 6148
  0.7 22.6 %copy-start.2 = (f32[16,512]{1,0:T(8,128)S(1)}, f32[16,512]{1,0:T(8,128)}, u32[]{:S(2)}) copy-start(f32[16,512]{1,0:T(8,128)} %param.26) | copy-start | bytes 98308
  21.7 4.5 %copy-start.5 = (f32[512]{0:T(512)S(1)}, f32[512]{0:T(512)}, u32[]{:S(2)}) copy-start(f32[512]{0:T(512)} %param.27) | copy-start | bytes 6148
  21.8 5.1 %copy-start.3 = (s32[8,2]{0,1:T(2,128)S(1)}, s32[8,2]{0,1:T(2,128)}, u32[]{:S(2)}) copy-start(s32[8,2]{0,1:T(2,128)} %param.31) | copy-start | bytes 196
  21.9 5.8 %copy-start.6 = (f32[8,2]{0,1:T(2,128)S(1)}, f32[8,2]{0,1:T(2,128)}, u32[]{:S(2)}) copy-start(f32[8,2]{0,1:T(2,128)} %param.32) | copy-start | bytes 196

commit v2 on v1

--- a/solution.py
+++ b/solution.py
@@ -10,6 +10,7 @@
 FLIGHT = 2
 CAP = 4
 PACK = 4
+CHUNKS = 4
 MESH = pl.DeviceIdType.MESH
 
 
@@ -98,7 +99,6 @@
     residual_ref,
     gain_ref,
     ids_ref,
-    ids_t_ref,
     route_ref,
     w_gate,
     w_up,
@@ -111,6 +111,8 @@
     part,
     own,
     pair_in,
+    side_out,
+    side_in,
     summed,
     mixed_in,
     hidden_ref,
@@ -125,7 +127,11 @@
     back_sum,
     final_in,
     local_sem,
-    pair_sem,
+    swap_sem,
+    pair_send,
+    pair_recv,
+    side_send,
+    side_recv,
     mixed_send,
     mixed_recv,
     rows_send,
@@ -164,64 +170,85 @@
     for load in loads:
         load.start()
 
-    tile = 512
+    lines = chips // 2
+    line, side = chip // 2, chip % 2
+    across = (line * 2 + 1 - side) * 2 + core
+    chunks = part.shape[0]
+    tile = width // chunks
     y_other = y_ref[other]
 
-    @pl.loop(0, width // tile)
-    def _(t):
-        cols = pl.ds(pl.multiple_of(t * tile, tile), tile)
-        value = jnp.dot(y_other, v_out[:, cols], preferred_element_type=f32)
-        part[:, :, cols] = value.reshape(chips, row_dev, tile).astype(bf16)
-
-    pl.semaphore_wait(barrier, chips)
-    pair = push(part, pair_in, pair_sem.at[0], pair_sem.at[1], partner)
-    pair.start()
+    def pair_copy(c):
+        return push(part.at[c], pair_in.at[c], pair_send.at[c], pair_recv.at[c], partner)
+
+    def side_copy(c):
+        return push(side_out.at[c], side_in.at[c], side_send.at[c], side_recv.at[c], across)
+
+    def mixed_copy(c, owner, sender, peer):
+        return push(
+            summed.at[c, owner], mixed_in.at[c, sender],
+            mixed_send.at[c, owner], mixed_recv.at[c, sender],
+            (peer * 2 + side) * 2 + core,
+        )
+
+    for c in range(chunks):
+        value = jnp.dot(
+            y_other, v_out[:, c * tile : (c + 1) * tile], preferred_element_type=f32
+        )
+        part[c] = value.reshape(lines, 2, row_dev, tile).astype(bf16)
+        if c == 0:
+            pl.semaphore_wait(barrier, chips)
+        pair_copy(c).start()
     y_own = y_ref[core]
-
-    @pl.loop(0, width // tile)
-    def _(t):
-        cols = pl.ds(pl.multiple_of(t * tile, tile), tile)
-        value = jnp.dot(y_own, v_out[:, cols], preferred_element_type=f32)
-        own[:, :, cols] = value.reshape(chips, row_dev, tile)
-
-    pair.wait_recv()
-
-    def mixed_copy(owner, sender):
-        return push(
-            summed.at[owner], mixed_in.at[sender], mixed_send.at[owner], mixed_recv.at[sender],
-            owner * 2 + core,
+    for c in range(chunks):
+        value = jnp.dot(y_own, v_out[:, c * tile : (c + 1) * tile], preferred_element_type=f32)
+        own[c] = value.reshape(lines, 2, row_dev, tile)
+        pair_copy(c).wait_recv()
+        side_out[c] = (own[c, :, 1 - side] + pair_in[c, :, 1 - side].astype(f32)).astype(bf16)
+        side_copy(c).start()
+    for c in range(chunks):
+        side_copy(c).wait_recv()
+
+        @pl.loop(1, lines)
+        def _(k):
+            owner = (line + k) % lines
+            summed[c, owner] = (
+                own[c, owner, side]
+                + pair_in[c, owner, side].astype(f32)
+                + side_in[c, owner].astype(f32)
+            ).astype(bf16)
+            mixed_copy(c, owner, line, owner).start()
+
+        cols = slice(c * tile, (c + 1) * tile)
+        hidden_ref[:, cols] = (
+            residual_ref[:, cols].astype(f32)
+            + own[c, line, side]
+            + pair_in[c, line, side].astype(f32)
+            + side_in[c, line].astype(f32)
         )
-
-    @pl.loop(1, chips)
-    def _(k):
-        owner = (chip + k) % chips
-        summed[owner] = (own[owner] + pair_in[owner].astype(f32)).astype(bf16)
-        mixed_copy(owner, chip).start()
-
-    hidden_ref[...] = residual_ref[...].astype(f32) + own[chip] + pair_in[chip].astype(f32)
-
-    @pl.loop(1, chips)
-    def _(k):
-        sender = (chip + chips - k) % chips
-        push(
-            summed.at[sender], mixed_in.at[sender], mixed_send.at[sender], mixed_recv.at[sender],
-            sender * 2 + core,
-        ).wait_recv()
-        hidden_ref[...] += mixed_in[sender].astype(f32)
+    for c in range(chunks):
+
+        @pl.loop(1, lines)
+        def _(k):
+            sender = (line + lines - k) % lines
+            mixed_copy(c, sender, sender, sender).wait_recv()
+            hidden_ref[:, c * tile : (c + 1) * tile] += mixed_in[c, sender].astype(f32)
 
     hidden = hidden_ref[...]
     scale = lax.rsqrt(jnp.mean(hidden * hidden, axis=-1, keepdims=True) + 1e-06)
     normed = (hidden * scale * gain_ref[...]).astype(bf16).astype(f32)
 
-    ids, ids_t, route = ids_ref[...], ids_t_ref[...], route_ref[...]
-    earlier = lax.broadcasted_iota(jnp.int32, (row_dev, row_dev), 1) < lax.broadcasted_iota(
-        jnp.int32, (row_dev, row_dev), 0
-    )
+    ids, route = ids_ref[...], route_ref[...]
+    at_row = lax.broadcasted_iota(jnp.int32, (row_dev, row_dev), 0)
+    at_col = lax.broadcasted_iota(jnp.int32, (row_dev, row_dev), 1)
+
+    def upright(values):
+        return jnp.sum(jnp.where(at_row == at_col, values, 0.0), axis=1, keepdims=True)
+
     masks = []
     for e in range(FLIGHT):
-        named = jnp.where((ids[:, 0:1] == e) | (ids[:, 1:2] == e), 1.0, 0.0)
-        named_row = jnp.where((ids_t[0:1, :] == e) | (ids_t[1:2, :] == e), 1.0, 0.0)
-        place = jnp.sum(jnp.where(earlier, named_row, 0.0), axis=1, keepdims=True)
+        named_row = jnp.where((ids[0:1, :] == e) | (ids[1:2, :] == e), 1.0, 0.0)
+        named = upright(named_row)
+        place = jnp.sum(jnp.where(at_col < at_row, named_row, 0.0), axis=1, keepdims=True)
         masks.append([jnp.where(place == float(r), named, 0.0) for r in range(CAP)])
         for r in range(CAP):
             row = jnp.sum(masks[e][r] * normed, axis=0, keepdims=True)
@@ -305,7 +332,7 @@
             back_f[...] += moved
     back[...] = back_f[...].reshape(2, chips, block, piece).astype(bf16)
 
-    swap = push(back.at[other], back_in, pair_sem.at[2], pair_sem.at[3], partner)
+    swap = push(back.at[other], back_in, swap_sem.at[0], swap_sem.at[1], partner)
     swap.start()
     swap.wait_recv()
 
@@ -330,7 +357,7 @@
 
     hidden = hidden_ref[...]
     for e in range(FLIGHT):
-        coef = jnp.sum(jnp.where(ids == e, route, 0.0), axis=1, keepdims=True)
+        coef = upright(jnp.sum(jnp.where(ids == e, route, 0.0), axis=0, keepdims=True))
         total = jnp.sum(final_in[e * half : (e + 1) * half].astype(f32), axis=0)
         weights = [coef * masks[e][r] for r in range(CAP)]
         if e == 0:
@@ -344,14 +371,21 @@
         cols = slice(q * piece, (q + 1) * piece)
         result_ref[:, cols] = (hidden[:, cols] + moe[q]).astype(bf16)
 
-    pair.wait_send()
+    for c in range(chunks):
+        pair_copy(c).wait_send()
+        side_copy(c).wait_send()
+
+        @pl.loop(1, lines)
+        def _(k):
+            owner = (line + k) % lines
+            mixed_copy(c, owner, line, owner).wait_send()
+
     swap.wait_send()
     rows_copy(core, chip, chip, other, my_expert, chip).wait_send()
 
     @pl.loop(1, chips)
     def _(k):
         peer = (chip + k) % chips
-        mixed_copy(peer, chip).wait_send()
         rows_copy(core, chip, peer, core, peer // half, peer).wait_send()
         forward(peer, core).wait_send()
         final_copy(peer, chip, peer).wait_send()
@@ -361,24 +395,27 @@
     chips = n // 2
     row_dev, width = residual.shape
     piece, block = width // PACK, CAP * PACK
+    lines, tile = chips // 2, width // CHUNKS
     vmem, hbm = pl.BlockSpec(memory_space=pltpu.VMEM), pl.BlockSpec(memory_space=pl.ANY)
     bf16, f32 = jnp.bfloat16, jnp.float32
     dma = pltpu.SemaphoreType.DMA
     return pl.pallas_call(
         functools.partial(moe_kernel, n),
         out_shape=jax.ShapeDtypeStruct((row_dev, width), bf16),
-        in_specs=[vmem, hbm, vmem, vmem, vmem, vmem, vmem, hbm, hbm, hbm],
+        in_specs=[vmem, hbm, vmem, vmem, vmem, vmem, hbm, hbm, hbm],
         out_specs=vmem,
         scratch_shapes=[
             pltpu.VMEM(out_weight.shape, bf16),
             pltpu.VMEM(w_gate.shape, bf16),
             pltpu.VMEM(w_up.shape, bf16),
             pltpu.VMEM(w_down.shape, bf16),
-            pltpu.VMEM((chips, row_dev, width), bf16),
-            pltpu.VMEM((chips, row_dev, width), f32),
-            pltpu.VMEM((chips, row_dev, width), bf16),
-            pltpu.VMEM((chips, row_dev, width), bf16),
-            pltpu.VMEM((chips, row_dev, width), bf16),
+            pltpu.VMEM((CHUNKS, lines, 2, row_dev, tile), bf16),
+            pltpu.VMEM((CHUNKS, lines, 2, row_dev, tile), f32),
+            pltpu.VMEM((CHUNKS, lines, 2, row_dev, tile), bf16),
+            pltpu.VMEM((CHUNKS, lines, row_dev, tile), bf16),
+            pltpu.VMEM((CHUNKS, lines, row_dev, tile), bf16),
+            pltpu.VMEM((CHUNKS, lines, row_dev, tile), bf16),
+            pltpu.VMEM((CHUNKS, lines, row_dev, tile), bf16),
             pltpu.VMEM((row_dev, width), f32),
             pltpu.VMEM((FLIGHT, block, piece), f32),
             pltpu.VMEM((FLIGHT, block, piece), bf16),
@@ -391,9 +428,13 @@
             pltpu.VMEM((chips, block, piece), bf16),
             pltpu.VMEM((chips, block, piece), bf16),
             dma((4,)),
-            dma((4,)),
-            dma((chips,)),
-            dma((chips,)),
+            dma((2,)),
+            dma((CHUNKS,)),
+            dma((CHUNKS,)),
+            dma((CHUNKS,)),
+            dma((CHUNKS,)),
+            dma((CHUNKS, lines)),
+            dma((CHUNKS, lines)),
             dma((chips,)),
             dma((n,)),
             dma((chips,)),
@@ -403,7 +444,7 @@
         compiler_params=pltpu.CompilerParams(
             collective_id=1, has_side_effects=True, vmem_limit_bytes=60 * 2**20
         ),
-    )(y, out_weight, residual, gain.reshape(1, width), ids, ids.T, route, w_gate, w_up, w_down)
+    )(y, out_weight, residual, gain.reshape(1, width), ids.T, route.T, w_gate, w_up, w_down)
 
 
 def shards(

time: 75.6 us -> 71.4 us (0.944)
  Pallas kernels: 62.4 us -> 58.8 us
  local copies, waits for them, and re-layouts: 4.79 us -> 3.32 us
  other arithmetic: 4.8 us -> 5.74 us
    pallas_call x1, Pallas kernels: 45.5 us -> 41.9 us  [mix_experts(): pl.pallas_call(functools.partial(moe_kernel, n), out_shape=jax.ShapeDtype...]
    unnamed x21 -> x13, local copies, waits for them, and re-layouts: 2.91 us -> 1.55 us
    neg x1, other arithmetic: 0.01 us -> 0.92 us  [shards(): rates = -jnp.exp(a_log)]
where the time goes in v2:
time: 71.4 us; the launch traced here: 71.1 us
  Pallas kernels  58.8 us (82%)
  other arithmetic  5.74 us (8%)
  local copies, waits for them, and re-layouts  3.32 us (5%)
  matrix products  2.48 us (3%)
  between operations  0.76 us (1%)
    pallas_call x1, Pallas kernels, mix_experts(): pl.pallas_call(functools.partial(moe_kernel, n), out_shape=jax.ShapeDtype...  41.9 us
    pallas_call x1, Pallas kernels, sum_proj(): pl.pallas_call(functools.partial(proj_kernel, n), out_shape=jax.ShapeDtyp...  16.9 us
    convert_element_type x1, other arithmetic, shards(): new_state = state.astype(jnp.bfloat16)  2.85 us
    unnamed x13, local copies, waits for them, and re-layouts  1.55 us
    slice x1, local copies, waits for them, and re-layouts, shards(): x_new = xz[:, 0, :].astype(jnp.float32)  1.53 us
    dot_general x1, matrix products, shards(): jnp.dot(dt_low, dt_weight, preferred_element_type=jnp.float32) + dt_bias  1.44 us

profile of v2, /device:TPU:0, one launch (start us, length us, event | category | flops | bytes accessed | tf_op | source)
XLA Modules:
  0.0 71.1 jit_solution(13119552389538787062)
XLA Ops:
  0.6 0.0 copy-start
  0.6 0.0 copy-start.2
  0.7 0.0 copy-start.4
  0.7 0.0 copy-start.1
  0.7 0.9 %exponential_negate_fusion = f32[16,512]{1,0:T(8,128)S(1)} fusion(f32[16,512]{1,0:T(8,128)} %param.26), kind=kLoop, calls=%fused_computation.20 | loop fusion | flops 8192 | bytes 65536 | tf_op jit(solution)/shard_map/neg | solution.py:488
  1.6 1.5 %fusion.9 = (bf16[128,1,512]{2,1,0:T(2,128)(2,1)S(1)}, bf16[128,1,512]{2,1,0:T(2,128)(2,1)S(1)}) fusion(bf16[128,2,512]{2,1,0:T(2,128)(2,1)} %param.18), kind=kLoop, calls=%fused_computation.23 | loop fusion | bytes 524288 | tf_op jit(solution)/shard_map/slice | solution.py:474
  3.2 1.1 %multiply_reduce_fusion.1 = f32[128,512]{1,0:T(8,128)S(1)} fusion(bf16[128,1,512]{2,0,1:T(8,128)(2,1)S(1)} %copy.29, bf16[128,3,512]{2,0,1:T(8,128)(2,1)} %param.19, f32[4,512]{1,0:T(4,128)} %param.20), kind=kLoop, calls=%fused_computation.5 | loop fusion | flops 983040 | bytes 794624 | tf_op jit(solution)/shard_map/reduce_sum | solution.py:477
  4.3 0.0 copy-done
  4.3 1.0 %convolution_convert_fusion = bf16[128,544]{0,1:T(8,128)(2,1)S(1)} fusion(bf16[512,544]{0,1:T(8,128)(2,1)S(1)} %copy-done, f32[128,512]{1,0:T(8,128)S(1)} %multiply_reduce_fusion.1, f32[512]{0:T(512)} %param.21), kind=kOutput, calls=%fused_computation.4 | convolution fusion | flops 71766016 | bytes 960512 | tf_op jit(solution)/shard_map/dot_general | solution.py:479
  5.4 0.2 copy.26
  5.5 16.9 %shard_map.185 = bf16[16,8,544]{2,1,0:T(8,128)(2,1)S(1)} custom-call(bf16[16,8,544]{2,1,0:T(8,128)(2,1)S(1)} %bitcast.17), custom_call_target="tpu_custom_call" | custom-call | tf_op jit(solution)/shard_map/pallas_call | solution.py:79
  22.5 0.0 copy-start.3
  22.5 0.1 fusion.8
  22.6 0.0 copy-done.2
  22.6 0.0 copy-done.4
  22.6 1.4 %convert_multiply_fusion.1 = (f32[128,512]{1,0:T(8,128)S(1)}, f32[128,512]{1,0:T(8,128)S(1)}) fusion(f32[128,512]{1,0:T(8,128)S(1)} %multiply_reduce_fusion.1, f32[512]{0:T(512)S(1)} %copy-done.2, f32[512]{0:T(512)S(1)} %copy-done.4, bf16[512,512]{1,0:T(8,128)(2,1)} %param.24, bf16[128,544]{1,0:T(8,128)(2,1)S(1)} %bitcast.18), kind=kOutput, calls=%fused_computation.14 | convolution fusion | flops 68091904 | bytes 1445888 | tf_op jit(solution)/shard_map/dot_general | solution.py:486
  24.1 0.0 copy-done.1
  24.1 2.8 %fusion = (bf16[128,16,512]{2,1,0:T(8,128)(2,1)}, f32[128,512]{1,0:T(8,128)S(1)}) fusion(bf16[128,16,512]{2,1,0:T(8,128)(2,1)S(1)} %copy-done.1, f32[128,16]{1,0:T(8,128)S(1)} %get-tuple-element.4, f32[128,512]{1,0:T(8,128)S(1)} %get-tuple-element.8, f32[16,512]{1,0:T(8,128)S(1)} %exponential_negate_fusion, f32[128,512]{1,0:T(8,128)S(1)} %get-tuple-element.9, ...), kind=kLoop, calls=%fused_computation.2 | loop fusion | flops 8323072 | bytes 5029888 | tf_op jit(solution)/shard_map/convert_element_type | solution.py:496
  26.9 0.0 copy-done.3
  26.9 0.8 %copy_bitcast_fusion.y_ref = bf16[2,64,512]{2,1,0:T(8,128)(2,1)} fusion(bf16[8,2,8,512]{3,2,1,0:T(8,128)(2,1)S(1)} %bitcast.21, f32[8,2,8,512]{3,2,1,0:T(8,128)S(1)} %bitcast.20, f32[8,2,8,512]{3,2,1,0:T(8,128)S(1)} %bitcast.19, f32[512]{0:T(512)S(1)} %copy-done.2, f32[512]{0:T(512)S(1)} %copy-done.3), kind=kLoop, calls=%fused_computation.18 | loop fusion | flops 1048576 | bytes 790528 | tf_op jit(solution)/shard_map/reshape | solution.py:499
  27.8 41.9 %shard_map.186 = bf16[8,4096]{1,0:T(8,128)(2,1)} custom-call(bf16[2,64,512]{2,1,0:T(8,128)(2,1)} %copy_bitcast_fusion.y_ref, bf16[512,4096]{1,0:T(8,128)(2,1)} %out_weight.1, bf16[8,4096]{1,0:T(8,128)(2,1)} %residual_ref.1, f32[1,4096]{1,0:T(1,128)} %bitcast.22, s32[2,8]{1,0:T(2,128)} %bitcast.23, f32[2,8]{1,0:T(2,128)} %bitcast.24, ...), custom_call_target="tpu_custom_call" | custom-call | tf_op jit(solution)/shard_map/pallas_call | solution.py:402
  69.6 1.5 %copy.33 = bf16[8,4096]{1,0:T(8,128)(2,1)} copy(bf16[8,4096]{1,0:T(8,128)(2,1)} %shard_map.186) | data formatting | bytes 131072
  (3 shorter events, 0.1 us)
Async XLA Ops:
  0.6 3.7 %copy-start = (bf16[512,544]{0,1:T(8,128)(2,1)S(1)}, bf16[512,544]{0,1:T(8,128)(2,1)}, u32[]{:S(2)}) copy-start(bf16[512,544]{0,1:T(8,128)(2,1)} %param.23) | copy-start | bytes 1671172
  0.6 22.0 %copy-start.2 = (f32[512]{0:T(512)S(1)}, f32[512]{0:T(512)}, u32[]{:S(2)}) copy-start(f32[512]{0:T(512)} %param.21) | copy-start | bytes 6148
  0.7 22.0 %copy-start.4 = (f32[512]{0:T(512)S(1)}, f32[512]{0:T(512)}, u32[]{:S(2)}) copy-start(f32[512]{0:T(512)} %param.25) | copy-start | bytes 6148
  0.7 23.4 %copy-start.1 = (bf16[128,16,512]{2,1,0:T(8,128)(2,1)S(1)}, bf16[128,16,512]{2,1,0:T(8,128)(2,1)}, u32[]{:S(2)}) copy-start(bf16[128,16,512]{2,1,0:T(8,128)(2,1)} %param.22) | copy-start | bytes 6291460
  22.5 4.5 %copy-start.3 = (f32[512]{0:T(512)S(1)}, f32[512]{0:T(512)}, u32[]{:S(2)}) copy-start(f32[512]{0:T(512)} %param.27) | copy-start | bytes 6148

commit v3 on v2

--- a/solution.py
+++ b/solution.py
@@ -25,67 +25,104 @@
     )
 
 
-def proj_kernel(n, part_ref, out_ref, landed, full, send_a, recv_a, send_b, recv_b):
+def proj_kernel(
+    chips, part_ref, out_ref, pair_in, summed, landed, full,
+    pair_sem, send_a, recv_a, send_b, recv_b, send_c, recv_c,
+):
     me = lax.axis_index("chan")
+    chip, core = me // 2, me % 2
+    other = 1 - core
+    partner = chip * 2 + other
     barrier = pltpu.get_barrier_semaphore()
-
-    @pl.loop(1, n)
-    def _(k):
-        pl.semaphore_signal(barrier, inc=1, device_id={"chan": (me + k) % n}, device_id_type=MESH)
-
-    pl.semaphore_wait(barrier, n - 1)
+    pl.semaphore_signal(barrier, inc=1, device_id={"chan": partner}, device_id_type=MESH)
+
+    @pl.loop(1, chips)
+    def _(k):
+        peer = ((chip + k) % chips) * 2 + core
+        pl.semaphore_signal(barrier, inc=1, device_id={"chan": peer}, device_id_type=MESH)
+
+    pl.semaphore_wait(barrier, chips)
+    pair = push(part_ref.at[other], pair_in, pair_sem.at[0], pair_sem.at[1], partner)
 
     def scatter(owner, sender, peer):
-        return push(part_ref.at[owner], landed.at[sender], send_a.at[owner], recv_a.at[sender], peer)
-
-    def gather(slot, peer, sem):
-        return push(full.at[slot], full.at[slot], send_b.at[sem], recv_b.at[slot], peer)
-
-    @pl.loop(1, n)
-    def _(k):
-        peer = (me + k) % n
-        scatter(peer, me, peer).start()
+        return push(
+            summed.at[owner], landed.at[sender], send_a.at[owner], recv_a.at[sender],
+            peer * 2 + core,
+        )
+
+    def gather(sender, peer):
+        here = full.at[sender, core]
+        return push(here, here, send_b.at[peer], recv_b.at[sender], peer * 2 + core)
+
+    def forward(sender, side):
+        here = full.at[sender, side]
+        return push(here, here, send_c.at[sender], recv_c.at[sender], partner)
+
+    pair.start()
+    pair.wait_recv()
+
+    @pl.loop(1, chips)
+    def _(k):
+        peer = (chip + k) % chips
+        summed[peer] = (
+            part_ref[core, peer].astype(jnp.float32) + pair_in[peer].astype(jnp.float32)
+        ).astype(jnp.bfloat16)
+        scatter(peer, chip, peer).start()
 
     def add(k, total):
-        peer = (me + n - k) % n
+        peer = (chip + chips - k) % chips
         scatter(peer, peer, peer).wait_recv()
         return total + landed[peer].astype(jnp.float32)
 
-    total = lax.fori_loop(1, n, add, part_ref[me].astype(jnp.float32))
-    full[me] = total.astype(jnp.bfloat16)
-
-    @pl.loop(1, n)
-    def _(k):
-        peer = (me + k) % n
-        gather(me, peer, peer).start()
-
-    @pl.loop(1, n)
-    def _(k):
-        peer = (me + n - k) % n
-        gather(peer, peer, peer).wait_recv()
+    total = lax.fori_loop(
+        1,
+        chips,
+        add,
+        part_ref[core, chip].astype(jnp.float32) + pair_in[chip].astype(jnp.float32),
+    )
+    full[chip, core] = total.astype(jnp.bfloat16)
+
+    @pl.loop(1, chips)
+    def _(k):
+        gather(chip, (chip + k) % chips).start()
+
+    forward(chip, core).start()
+
+    @pl.loop(1, chips)
+    def _(k):
+        sender = (chip + chips - k) % chips
+        gather(sender, sender).wait_recv()
+        forward(sender, core).start()
+
+    @pl.loop(0, chips)
+    def _(k):
+        sender = (chip + chips - k) % chips
+        forward(sender, other).wait_recv()
 
     out_ref[...] = full[...]
-
-    @pl.loop(1, n)
-    def _(k):
-        peer = (me + k) % n
-        scatter(peer, me, peer).wait_send()
-        gather(me, peer, peer).wait_send()
-
-
-def sum_proj(part, n):
-    rows, cols = part.shape[1:]
+    pair.wait_send()
+    forward(chip, core).wait_send()
+
+    @pl.loop(1, chips)
+    def _(k):
+        peer = (chip + k) % chips
+        scatter(peer, chip, peer).wait_send()
+        gather(chip, peer).wait_send()
+        forward(peer, core).wait_send()
+
+
+def sum_proj(part, chips):
+    rows, cols = part.shape[2:]
     vmem = pl.BlockSpec(memory_space=pltpu.VMEM)
+    dma = pltpu.SemaphoreType.DMA
     return pl.pallas_call(
-        functools.partial(proj_kernel, n),
-        out_shape=jax.ShapeDtypeStruct(part.shape, jnp.bfloat16),
+        functools.partial(proj_kernel, chips),
+        out_shape=jax.ShapeDtypeStruct((chips, 2, rows, cols), jnp.bfloat16),
         in_specs=[vmem],
         out_specs=vmem,
-        scratch_shapes=[
-            pltpu.VMEM((n, rows, cols), jnp.bfloat16),
-            pltpu.VMEM((n, rows, cols), jnp.bfloat16),
-        ]
-        + [pltpu.SemaphoreType.DMA((n,))] * 4,
+        scratch_shapes=[pltpu.VMEM((chips, rows, cols), jnp.bfloat16)] * 3
+        + [pltpu.VMEM((chips, 2, rows, cols), jnp.bfloat16), dma((2,))]
+        + [dma((chips,))] * 6,
         compiler_params=pltpu.CompilerParams(
             collective_id=0, has_side_effects=True, vmem_limit_bytes=16 * 2**20
         ),
@@ -477,7 +514,8 @@
     conv_out = jnp.sum(window * conv_weight[None, :, :], axis=1) + conv_bias
     u_mixer = jax.nn.silu(conv_out).astype(jnp.bfloat16)
     part = jnp.dot(u_mixer, x_weight, preferred_element_type=jnp.float32).astype(jnp.bfloat16)
-    proj = sum_proj(part.reshape(devices, row_dev, -1), devices).reshape(part.shape)
+    halves = part.reshape(devices // 2, 2, row_dev, -1).transpose(1, 0, 2, 3)
+    proj = sum_proj(halves, devices // 2).reshape(part.shape)
     proj = proj.astype(jnp.float32)
     dt_low = proj[:, :rank_cols].astype(jnp.bfloat16)
     b_in = proj[:, rank_cols : rank_cols + nstate]

time: 71.4 us -> 70.5 us (0.987)
  Pallas kernels: 58.8 us -> 57.8 us
    pallas_call x1, Pallas kernels: 41.9 us -> 41 us  [mix_experts(): pl.pallas_call(functools.partial(moe_kernel, n), out_shape=jax.ShapeDtype...]
where the time goes in v3:
time: 70.5 us; the launch traced here: 70.2 us
  Pallas kernels  57.8 us (82%)
  other arithmetic  5.66 us (8%)
  local copies, waits for them, and re-layouts  3.45 us (5%)
  matrix products  2.48 us (4%)
  between operations  0.77 us (1%)
    pallas_call x1, Pallas kernels, mix_experts(): pl.pallas_call(functools.partial(moe_kernel, n), out_shape=jax.ShapeDtype...  41 us
    pallas_call x1, Pallas kernels, sum_proj(): pl.pallas_call(functools.partial(proj_kernel, chips), out_shape=jax.Shape...  16.8 us
    convert_element_type x1, other arithmetic, shards(): new_state = state.astype(jnp.bfloat16)  2.85 us
    slice x1, local copies, waits for them, and re-layouts, shards(): x_new = xz[:, 0, :].astype(jnp.float32)  1.64 us
    unnamed x13, local copies, waits for them, and re-layouts  1.55 us
    dot_general x1, matrix products, shards(): jnp.dot(dt_low, dt_weight, preferred_element_type=jnp.float32) + dt_bias  1.44 us

profile of v3, /device:TPU:0, one launch (start us, length us, event | category | flops | bytes accessed | tf_op | source)
XLA Modules:
  0.0 70.2 jit_solution(17482609070733561168)
XLA Ops:
  0.6 0.0 copy-start
  0.6 0.0 copy-start.2
  0.7 0.0 copy-start.4
  0.7 0.8 %exponential_negate_fusion = f32[16,512]{1,0:T(8,128)S(1)} fusion(f32[16,512]{1,0:T(8,128)} %param.26), kind=kLoop, calls=%fused_computation.21 | loop fusion | flops 8192 | bytes 65536 | tf_op jit(solution)/shard_map/neg | solution.py:526
  1.5 0.0 copy-start.1
  1.5 1.6 %fusion.9 = (bf16[128,1,512]{2,1,0:T(2,128)(2,1)S(1)}, bf16[128,1,512]{2,1,0:T(2,128)(2,1)S(1)}) fusion(bf16[128,2,512]{2,1,0:T(2,128)(2,1)} %param.18), kind=kLoop, calls=%fused_computation.24 | loop fusion | bytes 524288 | tf_op jit(solution)/shard_map/slice | solution.py:511
  3.2 1.1 %multiply_reduce_fusion.1 = f32[128,512]{1,0:T(8,128)S(1)} fusion(bf16[128,1,512]{2,0,1:T(8,128)(2,1)S(1)} %copy.29, bf16[128,3,512]{2,0,1:T(8,128)(2,1)} %param.19, f32[4,512]{1,0:T(4,128)} %param.20), kind=kLoop, calls=%fused_computation.5 | loop fusion | flops 983040 | bytes 794624 | tf_op jit(solution)/shard_map/reduce_sum | solution.py:514
  4.4 0.0 copy-done
  4.4 1.0 %convolution_convert_fusion = bf16[128,544]{0,1:T(8,128)(2,1)S(1)} fusion(bf16[512,544]{0,1:T(8,128)(2,1)S(1)} %copy-done, f32[128,512]{1,0:T(8,128)S(1)} %multiply_reduce_fusion.1, f32[512]{0:T(512)} %param.21), kind=kOutput, calls=%fused_computation.4 | convolution fusion | flops 71766016 | bytes 960512 | tf_op jit(solution)/shard_map/dot_general | solution.py:516
  5.4 0.2 copy.25
  5.6 16.8 %shard_map.185 = bf16[8,2,8,544]{3,2,1,0:T(8,128)(2,1)S(1)} custom-call(bf16[2,8,8,544]{3,2,1,0:T(8,128)(2,1)S(1)} %bitcast.20), custom_call_target="tpu_custom_call" | custom-call | tf_op jit(solution)/shard_map/pallas_call | solution.py:118
  22.4 0.0 copy-start.3
  22.5 0.1 fusion.8
  22.5 0.0 copy-done.2
  22.5 0.0 copy-done.4
  22.6 1.4 %convert_multiply_fusion.1 = (f32[128,512]{1,0:T(8,128)S(1)}, f32[128,512]{1,0:T(8,128)S(1)}) fusion(f32[128,512]{1,0:T(8,128)S(1)} %multiply_reduce_fusion.1, f32[512]{0:T(512)S(1)} %copy-done.2, f32[512]{0:T(512)S(1)} %copy-done.4, bf16[512,512]{1,0:T(8,128)(2,1)} %param.24, bf16[128,544]{1,0:T(8,128)(2,1)S(1)} %bitcast.21), kind=kOutput, calls=%fused_computation.14 | convolution fusion | flops 68091904 | bytes 1445888 | tf_op jit(solution)/shard_map/dot_general | solution.py:524
  24.0 0.0 copy-done.1
  24.0 2.8 %fusion = (bf16[128,16,512]{2,1,0:T(8,128)(2,1)}, f32[128,512]{1,0:T(8,128)S(1)}) fusion(bf16[128,16,512]{2,1,0:T(8,128)(2,1)S(1)} %copy-done.1, f32[128,16]{1,0:T(8,128)S(1)} %get-tuple-element.4, f32[128,512]{1,0:T(8,128)S(1)} %get-tuple-element.8, f32[16,512]{1,0:T(8,128)S(1)} %exponential_negate_fusion, f32[128,512]{1,0:T(8,128)S(1)} %get-tuple-element.9, ...), kind=kLoop, calls=%fused_computation.2 | loop fusion | flops 8323072 | bytes 5029888 | tf_op jit(solution)/shard_map/convert_element_type | solution.py:534
  26.9 0.0 copy-done.3
  26.9 0.8 %copy_bitcast_fusion.1.y_ref = bf16[2,64,512]{2,1,0:T(8,128)(2,1)} fusion(bf16[8,2,8,512]{3,2,1,0:T(8,128)(2,1)S(1)} %bitcast.25, f32[8,2,8,512]{3,2,1,0:T(8,128)S(1)} %bitcast.23, f32[8,2,8,512]{3,2,1,0:T(8,128)S(1)} %bitcast.22, f32[512]{0:T(512)S(1)} %copy-done.2, f32[512]{0:T(512)S(1)} %copy-done.3), kind=kLoop, calls=%fused_computation.19 | loop fusion | flops 1048576 | bytes 790528 | tf_op jit(solution)/shard_map/reshape | solution.py:537
  27.7 41.0 %shard_map.186 = bf16[8,4096]{1,0:T(8,128)(2,1)} custom-call(bf16[2,64,512]{2,1,0:T(8,128)(2,1)} %copy_bitcast_fusion.1.y_ref, bf16[512,4096]{1,0:T(8,128)(2,1)} %out_weight.1, bf16[8,4096]{1,0:T(8,128)(2,1)} %residual_ref.1, f32[1,4096]{1,0:T(1,128)} %bitcast.26, s32[2,8]{1,0:T(2,128)} %bitcast.27, f32[2,8]{1,0:T(2,128)} %bitcast.28, ...), custom_call_target="tpu_custom_call" | custom-call | tf_op jit(solution)/shard_map/pallas_call | solution.py:439
  68.7 1.5 %copy.35 = bf16[8,4096]{1,0:T(8,128)(2,1)} copy(bf16[8,4096]{1,0:T(8,128)(2,1)} %shard_map.186) | data formatting | bytes 131072
  (4 shorter events, 0.1 us)
Async XLA Ops:
  0.6 3.7 %copy-start = (bf16[512,544]{0,1:T(8,128)(2,1)S(1)}, bf16[512,544]{0,1:T(8,128)(2,1)}, u32[]{:S(2)}) copy-start(bf16[512,544]{0,1:T(8,128)(2,1)} %param.23) | copy-start | bytes 1671172
  0.6 21.9 %copy-start.2 = (f32[512]{0:T(512)S(1)}, f32[512]{0:T(512)}, u32[]{:S(2)}) copy-start(f32[512]{0:T(512)} %param.21) | copy-start | bytes 6148
  0.7 21.9 %copy-start.4 = (f32[512]{0:T(512)S(1)}, f32[512]{0:T(512)}, u32[]{:S(2)}) copy-start(f32[512]{0:T(512)} %param.25) | copy-start | bytes 6148
  1.5 22.5 %copy-start.1 = (bf16[128,16,512]{2,1,0:T(8,128)(2,1)S(1)}, bf16[128,16,512]{2,1,0:T(8,128)(2,1)}, u32[]{:S(2)}) copy-start(bf16[128,16,512]{2,1,0:T(8,128)(2,1)} %param.22) | copy-start | bytes 6291460
  22.4 4.5 %copy-start.3 = (f32[512]{0:T(512)S(1)}, f32[512]{0:T(512)}, u32[]{:S(2)}) copy-start(f32[512]{0:T(512)} %param.27) | copy-start | bytes 6148

commit v4 on v3

--- a/solution.py
+++ b/solution.py
@@ -349,9 +349,8 @@
     units = v_gate.shape[1]
     span = 512 if units % 512 == 0 else units
 
-    @pl.loop(0, units // span)
-    def _(t):
-        cols = pl.ds(pl.multiple_of(t * span, span), span)
+    for t in range(units // span):
+        cols = slice(t * span, (t + 1) * span)
         gate = jnp.dot(rows[...], v_gate[:, cols], preferred_element_type=f32)
         upper = jnp.dot(rows[...], v_up[:, cols], preferred_element_type=f32)
         act[:, cols] = (jax.nn.silu(gate) * upper).astype(bf16)

time: 70.5 us -> 70.2 us (level)
  no operation moved by 1% of the time
where the time goes in v4:
time: 70.2 us; the launch traced here: 69.9 us
  Pallas kernels  57.5 us (82%)
  other arithmetic  5.66 us (8%)
  local copies, waits for them, and re-layouts  3.45 us (5%)
  matrix products  2.48 us (4%)
  between operations  0.77 us (1%)
    pallas_call x1, Pallas kernels, mix_experts(): pl.pallas_call(functools.partial(moe_kernel, n), out_shape=jax.ShapeDtype...  40.7 us
    pallas_call x1, Pallas kernels, sum_proj(): pl.pallas_call(functools.partial(proj_kernel, chips), out_shape=jax.Shape...  16.8 us
    convert_element_type x1, other arithmetic, shards(): new_state = state.astype(jnp.bfloat16)  2.85 us
    slice x1, local copies, waits for them, and re-layouts, shards(): x_new = xz[:, 0, :].astype(jnp.float32)  1.64 us
    unnamed x13, local copies, waits for them, and re-layouts  1.55 us
    dot_general x1, matrix products, shards(): jnp.dot(dt_low, dt_weight, preferred_element_type=jnp.float32) + dt_bias  1.44 us

profile of v4, /device:TPU:0, one launch (start us, length us, event | category | flops | bytes accessed | tf_op | source)
XLA Modules:
  0.0 69.9 jit_solution(10750998684406822939)
XLA Ops:
  0.6 0.0 copy-start
  0.6 0.0 copy-start.2
  0.7 0.0 copy-start.4
  0.7 0.8 %exponential_negate_fusion = f32[16,512]{1,0:T(8,128)S(1)} fusion(f32[16,512]{1,0:T(8,128)} %param.26), kind=kLoop, calls=%fused_computation.21 | loop fusion | flops 8192 | bytes 65536 | tf_op jit(solution)/shard_map/neg | solution.py:525
  1.5 0.0 copy-start.1
  1.5 1.6 %fusion.9 = (bf16[128,1,512]{2,1,0:T(2,128)(2,1)S(1)}, bf16[128,1,512]{2,1,0:T(2,128)(2,1)S(1)}) fusion(bf16[128,2,512]{2,1,0:T(2,128)(2,1)} %param.18), kind=kLoop, calls=%fused_computation.24 | loop fusion | bytes 524288 | tf_op jit(solution)/shard_map/slice | solution.py:510
  3.2 1.1 %multiply_reduce_fusion.1 = f32[128,512]{1,0:T(8,128)S(1)} fusion(bf16[128,1,512]{2,0,1:T(8,128)(2,1)S(1)} %copy.29, bf16[128,3,512]{2,0,1:T(8,128)(2,1)} %param.19, f32[4,512]{1,0:T(4,128)} %param.20), kind=kLoop, calls=%fused_computation.5 | loop fusion | flops 983040 | bytes 794624 | tf_op jit(solution)/shard_map/reduce_sum | solution.py:513
  4.4 0.0 copy-done
  4.4 1.0 %convolution_convert_fusion = bf16[128,544]{0,1:T(8,128)(2,1)S(1)} fusion(bf16[512,544]{0,1:T(8,128)(2,1)S(1)} %copy-done, f32[128,512]{1,0:T(8,128)S(1)} %multiply_reduce_fusion.1, f32[512]{0:T(512)} %param.21), kind=kOutput, calls=%fused_computation.4 | convolution fusion | flops 71766016 | bytes 960512 | tf_op jit(solution)/shard_map/dot_general | solution.py:515
  5.4 0.2 copy.25
  5.6 16.8 %shard_map.185 = bf16[8,2,8,544]{3,2,1,0:T(8,128)(2,1)S(1)} custom-call(bf16[2,8,8,544]{3,2,1,0:T(8,128)(2,1)S(1)} %bitcast.20), custom_call_target="tpu_custom_call" | custom-call | tf_op jit(solution)/shard_map/pallas_call | solution.py:118
  22.4 0.0 copy-start.3
  22.5 0.1 fusion.8
  22.5 0.0 copy-done.2
  22.5 0.0 copy-done.4
  22.6 1.4 %convert_multiply_fusion.1 = (f32[128,512]{1,0:T(8,128)S(1)}, f32[128,512]{1,0:T(8,128)S(1)}) fusion(f32[128,512]{1,0:T(8,128)S(1)} %multiply_reduce_fusion.1, f32[512]{0:T(512)S(1)} %copy-done.2, f32[512]{0:T(512)S(1)} %copy-done.4, bf16[512,512]{1,0:T(8,128)(2,1)} %param.24, bf16[128,544]{1,0:T(8,128)(2,1)S(1)} %bitcast.21), kind=kOutput, calls=%fused_computation.14 | convolution fusion | flops 68091904 | bytes 1445888 | tf_op jit(solution)/shard_map/dot_general | solution.py:523
  24.0 0.0 copy-done.1
  24.0 2.8 %fusion = (bf16[128,16,512]{2,1,0:T(8,128)(2,1)}, f32[128,512]{1,0:T(8,128)S(1)}) fusion(bf16[128,16,512]{2,1,0:T(8,128)(2,1)S(1)} %copy-done.1, f32[128,16]{1,0:T(8,128)S(1)} %get-tuple-element.4, f32[128,512]{1,0:T(8,128)S(1)} %get-tuple-element.8, f32[16,512]{1,0:T(8,128)S(1)} %exponential_negate_fusion, f32[128,512]{1,0:T(8,128)S(1)} %get-tuple-element.9, ...), kind=kLoop, calls=%fused_computation.2 | loop fusion | flops 8323072 | bytes 5029888 | tf_op jit(solution)/shard_map/convert_element_type | solution.py:533
  26.9 0.0 copy-done.3
  26.9 0.8 %copy_bitcast_fusion.1.y_ref = bf16[2,64,512]{2,1,0:T(8,128)(2,1)} fusion(bf16[8,2,8,512]{3,2,1,0:T(8,128)(2,1)S(1)} %bitcast.25, f32[8,2,8,512]{3,2,1,0:T(8,128)S(1)} %bitcast.23, f32[8,2,8,512]{3,2,1,0:T(8,128)S(1)} %bitcast.22, f32[512]{0:T(512)S(1)} %copy-done.2, f32[512]{0:T(512)S(1)} %copy-done.3), kind=kLoop, calls=%fused_computation.19 | loop fusion | flops 1048576 | bytes 790528 | tf_op jit(solution)/shard_map/reshape | solution.py:536
  27.7 40.7 %shard_map.186 = bf16[8,4096]{1,0:T(8,128)(2,1)} custom-call(bf16[2,64,512]{2,1,0:T(8,128)(2,1)} %copy_bitcast_fusion.1.y_ref, bf16[512,4096]{1,0:T(8,128)(2,1)} %out_weight.1, bf16[8,4096]{1,0:T(8,128)(2,1)} %residual_ref.1, f32[1,4096]{1,0:T(1,128)} %bitcast.26, s32[2,8]{1,0:T(2,128)} %bitcast.27, f32[2,8]{1,0:T(2,128)} %bitcast.28, ...), custom_call_target="tpu_custom_call" | custom-call | tf_op jit(solution)/shard_map/pallas_call | solution.py:438
  68.4 1.5 %copy.35 = bf16[8,4096]{1,0:T(8,128)(2,1)} copy(bf16[8,4096]{1,0:T(8,128)(2,1)} %shard_map.186) | data formatting | bytes 131072
  (4 shorter events, 0.1 us)
Async XLA Ops:
  0.6 3.7 %copy-start = (bf16[512,544]{0,1:T(8,128)(2,1)S(1)}, bf16[512,544]{0,1:T(8,128)(2,1)}, u32[]{:S(2)}) copy-start(bf16[512,544]{0,1:T(8,128)(2,1)} %param.23) | copy-start | bytes 1671172
  0.6 21.9 %copy-start.2 = (f32[512]{0:T(512)S(1)}, f32[512]{0:T(512)}, u32[]{:S(2)}) copy-start(f32[512]{0:T(512)} %param.21) | copy-start | bytes 6148
  0.7 21.9 %copy-start.4 = (f32[512]{0:T(512)S(1)}, f32[512]{0:T(512)}, u32[]{:S(2)}) copy-start(f32[512]{0:T(512)} %param.25) | copy-start | bytes 6148
  1.5 22.5 %copy-start.1 = (bf16[128,16,512]{2,1,0:T(8,128)(2,1)S(1)}, bf16[128,16,512]{2,1,0:T(8,128)(2,1)}, u32[]{:S(2)}) copy-start(bf16[128,16,512]{2,1,0:T(8,128)(2,1)} %param.22) | copy-start | bytes 6291460
  22.4 4.5 %copy-start.3 = (f32[512]{0:T(512)S(1)}, f32[512]{0:T(512)}, u32[]{:S(2)}) copy-start(f32[512]{0:T(512)} %param.27) | copy-start | bytes 6148
